TPU v7x, 32 devices: a whole 2x2x4 slice. The times are simulated.
32 devices in a mesh: groups: 2 (over y), tm: 4 (over z), tile: 2 (over x), arrow: 2 (over core).
Axes of the slice: x: 2, y: 2, z: 4, core: 2. Of those that a mesh axis runs over, the one named last changes fastest.
Arguments:
- forward_blocks: float32 [8, 96, 1024], P(('groups', 'tm'), ('tile', 'arrow')), parts along dimension 0, may hold values from -3 to 3
- arrow_rhs: float32 [192, 64], P(('groups', 'tile', 'arrow')), parts along dimension 0, may hold values from -6 to 6
- diag_inverse: bfloat16 [8, 1024, 1024], P(('groups', 'tm'), None, ('tile', 'arrow')), parts along dimension 0
- lower_coupling: bfloat16 [8, 1024, 1024], P(('groups', 'tm'), None, ('tile', 'arrow')), parts along dimension 0
- arrow_slab: bfloat16 [8, 64, 1024], P(('groups', 'tm'), 'arrow'), parts along dimension 0, may hold values from -0.09375 to 0.09375
- arrow_inverse: float32 [128, 64], P('groups'), parts along dimension 0
- boundary_term: float32 [192, 1024], P(('groups', 'tile', 'arrow')), parts along dimension 0, may hold values from -6 to 6
Outputs:
- solution: float32 [8, 96, 1024], P(('groups', 'tm'), ('tile', 'arrow')), parts along dimension 0
- arrow_solution: float32 [192, 64], P(('groups', 'tile', 'arrow')), parts along dimension 0
There are 2 independent parts, one for each index of `groups`. A program takes and returns all parts, laid end to end along the dimension named above; each array names one. Nothing has to cross between parts.
All inputs are finite; a program needn't handle non-finite values.
Results may differ from a plain program's by a relative error of at most 0.007.
Values may be sent and summed in bfloat16 or wider, within the bound.
A program may use at most 64 MiB of HBM per device.

v0:
```python
import jax
import jax.numpy as jnp
from jax import lax
from jax.sharding import PartitionSpec as P


def from_behind(block, axis, distance):
    devices = range(lax.axis_size(axis))
    route = [(i - distance, i) for i in devices if i - distance in devices]
    return lax.ppermute(block, axis, route)


def shards(
    forward_blocks,
    arrow_rhs,
    diag_inverse,
    lower_coupling,
    arrow_slab,
    arrow_inverse,
    boundary_term,
):
    highest = lax.Precision.HIGHEST
    slab_full = lax.all_gather(arrow_slab, "arrow", axis=1, tiled=True)
    slab_wide = slab_full[0].astype(jnp.float32)
    block_rows = forward_blocks[0]
    local_part = jnp.dot(block_rows, slab_wide.T, precision=highest)
    arrow_sum = lax.psum(local_part, "tm")
    arrow_forward = jnp.dot(arrow_rhs - arrow_sum, arrow_inverse.T, precision=highest)
    arrow_solution = jnp.dot(arrow_forward, arrow_inverse, precision=highest)
    arrow_term = jnp.dot(arrow_solution, slab_wide, precision=highest)
    source_rows = block_rows - arrow_term
    inverse_full, lower_full = (
        lax.all_gather(diag_inverse, ("tile", "arrow"), axis=2, tiled=True),
        lax.all_gather(lower_coupling, ("tile", "arrow"), axis=2, tiled=True),
    )
    coupling = jnp.dot(inverse_full[0], lower_full[0], preferred_element_type=jnp.float32).astype(
        jnp.bfloat16
    )
    coupling_wide = coupling.astype(jnp.float32)
    is_last = (lax.axis_index("tm") == lax.axis_size("tm") - 1).astype(jnp.float32)
    entry_term = is_last * boundary_term

    def one_turn(turn_index, carry_in):
        residual = source_rows - carry_in
        outgoing = jnp.dot(residual, coupling_wide, precision=highest)
        return entry_term + from_behind(outgoing, "tm", -1)

    carry_in = lax.fori_loop(0, lax.axis_size("tm") - 1, one_turn, entry_term)
    residual = source_rows - carry_in
    solution = jnp.dot(
        residual.astype(jnp.bfloat16), inverse_full[0], preferred_element_type=jnp.float32
    )
    return (solution[None], arrow_solution)


def solution(mesh):
    return jax.shard_map(
        shards,
        mesh=mesh,
        in_specs=(
            P(("groups", "tm"), ("tile", "arrow"), None),
            P(("groups", "tile", "arrow"), None),
            P(("groups", "tm"), None, ("tile", "arrow")),
            P(("groups", "tm"), None, ("tile", "arrow")),
            P(("groups", "tm"), "arrow", None),
            P("groups", None),
            P(("groups", "tile", "arrow"), None),
        ),
        out_specs=(
            P(("groups", "tm"), ("tile", "arrow"), None),
            P(("groups", "tile", "arrow"), None),
        ),
        check_vma=False,
    )
```

profile of v0, /device:TPU:0, one launch (start us, length us, event | category | flops | bytes accessed | tf_op | source)
XLA Modules:
  0.0 106.9 jit_solution(2100586051761688842)
XLA Ops:
  7.2 0.0 copy-start
  7.2 0.0 copy-start.2
  7.2 0.0 all-gather.3.cloned.1.call-start
  7.2 0.7 all-gather.3.cloned.1.call-update
  7.9 0.0 all-gather.5.cloned.1.call-start
  8.0 0.7 all-gather.5.cloned.1.call-update
  8.7 0.9 broadcast_multiply_fusion
  9.6 2.2 %all_gather.9 = bf16[1,64,1024]{2,1,0:T(8,128)(2,1)S(1)} all-gather(bf16[1,32,1024]{2,1,0:T(8,128)(2,1)} %param.13), channel_id=1, replica_groups=mesh['groups'=2,'tm'=4,'tile'=2,'arrow'=2] {'arrow'}, dimensions={1}, use_global_device_ids=true | all-gather | bytes 196608 | tf_op jit(solution)/shard_map/all_gather | solution.py:23
  11.8 1.1 fusion.15
  12.9 20.3 %psum.7 = f32[24,64]{1,0:T(8,128)S(1)} all-reduce(f32[24,64]{1,0:T(8,128)S(1)} %fusion.15), channel_id=1, replica_groups=mesh['groups'=2,'tm'=4,'tile'=2,'arrow'=2] {'tm'}, use_global_device_ids=true, to_apply=%region_0.0 | all-reduce | flops 1536 | bytes 12288 | tf_op jit(solution)/shard_map/psum | solution.py:27
  33.2 0.0 copy-done
  33.2 0.9 fusion.18
  34.1 0.2 fusion.20
  34.2 0.0 copy-done.2
  34.3 0.0 copy-start.3
  34.3 0.2 convolution_subtract_fusion
  34.5 0.7 all-gather.3.cloned.1.call-done
  35.1 24.4 %all-gather.5.cloned.1.call-done = bf16[1,1024,1024]{2,1,0:T(8,128)(2,1)} async-done(((bf16[1,1024,256]{2,1,0:T(8,128)(2,1)}), bf16[1,1024,1024]{2,1,0:T(8,128)(2,1)}) %all-gather.5.cloned.1.call-update) | async-done | bytes 2097168 | tf_op jit(solution)/shard_map/all_gather | solution.py:34
  59.6 6.5 %convert_convert_fusion = f32[1024,1024]{1,0:T(8,128)} fusion(bf16[1,1024,1024]{2,1,0:T(8,128)(2,1)} %all-gather.5.cloned.1.call-done, bf16[1,1024,1024]{2,1,0:T(8,128)(2,1)} %all-gather.3.cloned.1.call-done), kind=kOutput, calls=%fused_computation.7 | convolution fusion | flops 2149580800 | bytes 8388608 | tf_op jit(solution)/shard_map/dot_general | solution.py:36
  66.1 0.0 copy-done.3
  66.1 0.0 copy-start.1
  66.1 32.9 %while.10 = (s32[]{:T(128)}, f32[24,1024]{1,0:T(8,128)S(1)}, f32[24,1024]{1,0:T(8,128)S(1)}, f32[1024,1024]{1,0:T(8,128)}, f32[24,1024]{1,0:T(8,128)S(1)}, /*index=5*/s32[]{:T(128)}) while((s32[]{:T(128)}, f32[24,1024]{1,0:T(8,128)S(1)}, f32[24,1024]{1,0:T(8,128)S(1)}, f32[1024,1024]{1,0:T(8,128)}, f32[24,1024]{1,0:T(8,128)S(1)}, ...), condition=%wide.region_2.0_spmd, body=%wide.region_1.0_spmd.sunk | while | flops 302039040 | bytes 5177453 | solution.py:48
  66.1 4.4 %fusion.31 = f32[24,1024]{1,0:T(8,128)S(1)} fusion(f32[1024,1024]{1,0:T(8,128)} %get-tuple-element.86, f32[24,1024]{1,0:T(8,128)S(1)} %get-tuple-element.85, f32[24,1024]{1,0:T(8,128)S(1)} %get-tuple-element.78), kind=kOutput, calls=%fused_computation.clone.1 | convolution fusion | flops 302014464 | bytes 4489216 | tf_op jit(solution)/shard_map/while/body/eval_jaxpr/dot_general | solution.py:45
  70.5 1.3 %collective-permute-start = (f32[24,1024]{1,0:T(8,128)S(1)}, f32[24,1024]{1,0:T(8,128)S(1)}, u32[]{:S(2)}, u32[]{:S(2)}) collective-permute-start(f32[24,1024]{1,0:T(8,128)S(1)} %fusion.31), channel_id=1, source_target_pairs={{4,0},{8,4},{12,8},{5,1},{9,5},{13,9},{6,2},{10,6},{14,10},{7,3},{... | collective-permute-start | bytes 294920 | tf_op jit(solution)/shard_map/while/body/eval_jaxpr/ppermute | solution.py:10
  71.8 5.6 %collective-permute-done = f32[24,1024]{1,0:T(8,128)S(1)} collective-permute-done((f32[24,1024]{1,0:T(8,128)S(1)}, f32[24,1024]{1,0:T(8,128)S(1)}, u32[]{:S(2)}, u32[]{:S(2)}) %collective-permute-start) | collective-permute-done | bytes 98336 | tf_op jit(solution)/shard_map/while/body/eval_jaxpr/ppermute | solution.py:10
  77.4 4.3 %fusion.31 = f32[24,1024]{1,0:T(8,128)S(1)} fusion(f32[1024,1024]{1,0:T(8,128)} %get-tuple-element.86, f32[24,1024]{1,0:T(8,128)S(1)} %get-tuple-element.85, f32[24,1024]{1,0:T(8,128)S(1)} %get-tuple-element.78), kind=kOutput, calls=%fused_computation.clone.1 | convolution fusion | flops 302014464 | bytes 4489216 | tf_op jit(solution)/shard_map/while/body/eval_jaxpr/dot_general | solution.py:45
  81.7 1.3 %collective-permute-start = (f32[24,1024]{1,0:T(8,128)S(1)}, f32[24,1024]{1,0:T(8,128)S(1)}, u32[]{:S(2)}, u32[]{:S(2)}) collective-permute-start(f32[24,1024]{1,0:T(8,128)S(1)} %fusion.31), channel_id=1, source_target_pairs={{4,0},{8,4},{12,8},{5,1},{9,5},{13,9},{6,2},{10,6},{14,10},{7,3},{... | collective-permute-start | bytes 294920 | tf_op jit(solution)/shard_map/while/body/eval_jaxpr/ppermute | solution.py:10
  83.0 5.2 %collective-permute-done = f32[24,1024]{1,0:T(8,128)S(1)} collective-permute-done((f32[24,1024]{1,0:T(8,128)S(1)}, f32[24,1024]{1,0:T(8,128)S(1)}, u32[]{:S(2)}, u32[]{:S(2)}) %collective-permute-start) | collective-permute-done | bytes 98336 | tf_op jit(solution)/shard_map/while/body/eval_jaxpr/ppermute | solution.py:10
  88.2 4.3 %fusion.31 = f32[24,1024]{1,0:T(8,128)S(1)} fusion(f32[1024,1024]{1,0:T(8,128)} %get-tuple-element.86, f32[24,1024]{1,0:T(8,128)S(1)} %get-tuple-element.85, f32[24,1024]{1,0:T(8,128)S(1)} %get-tuple-element.78), kind=kOutput, calls=%fused_computation.clone.1 | convolution fusion | flops 302014464 | bytes 4489216 | tf_op jit(solution)/shard_map/while/body/eval_jaxpr/dot_general | solution.py:45
  92.5 1.3 %collective-permute-start = (f32[24,1024]{1,0:T(8,128)S(1)}, f32[24,1024]{1,0:T(8,128)S(1)}, u32[]{:S(2)}, u32[]{:S(2)}) collective-permute-start(f32[24,1024]{1,0:T(8,128)S(1)} %fusion.31), channel_id=1, source_target_pairs={{4,0},{8,4},{12,8},{5,1},{9,5},{13,9},{6,2},{10,6},{14,10},{7,3},{... | collective-permute-start | bytes 294920 | tf_op jit(solution)/shard_map/while/body/eval_jaxpr/ppermute | solution.py:10
  93.8 5.2 %collective-permute-done = f32[24,1024]{1,0:T(8,128)S(1)} collective-permute-done((f32[24,1024]{1,0:T(8,128)S(1)}, f32[24,1024]{1,0:T(8,128)S(1)}, u32[]{:S(2)}, u32[]{:S(2)}) %collective-permute-start) | collective-permute-done | bytes 98336 | tf_op jit(solution)/shard_map/while/body/eval_jaxpr/ppermute | solution.py:10
  99.0 0.0 copy-done.1
  99.0 1.0 fusion.11
  (4 shorter events, 0.0 us)
Async XLA Ops:
  7.2 26.0 %copy-start = (f32[64,64]{1,0:T(8,128)S(1)}, f32[64,64]{1,0:T(8,128)}, u32[]{:S(2)}) copy-start(f32[64,64]{1,0:T(8,128)} %param.14) | copy-start | bytes 49156
  7.2 27.1 %copy-start.2 = (f32[1,24,1024]{2,1,0:T(8,128)S(1)}, f32[1,24,1024]{2,1,0:T(8,128)}, u32[]{:S(2)}) copy-start(f32[1,24,1024]{2,1,0:T(8,128)} %param.9) | copy-start | bytes 294916
  7.2 28.0 %all-gather.3.cloned.1.call-start = ((), (), s32[]{:S(2)}) async-start(), calls=%async_computation | async-start | bytes 2621440 | tf_op jit(solution)/shard_map/all_gather | solution.py:33
  7.9 51.6 %all-gather.5.cloned.1.call-start = ((), (), s32[]{:S(2)}) async-start(), calls=%async_computation.1 | async-start | bytes 2621440 | tf_op jit(solution)/shard_map/all_gather | solution.py:34
  34.3 31.8 %copy-start.3 = (f32[24,64]{1,0:T(8,128)}, f32[24,64]{1,0:T(8,128)S(1)}, u32[]{:S(2)}) copy-start(f32[24,64]{1,0:T(8,128)S(1)} %fusion.20) | copy-start | bytes 18436
  66.1 33.0 %copy-start.1 = (bf16[1,1024,1024]{2,1,0:T(8,128)(2,1)S(1)}, bf16[1,1024,1024]{2,1,0:T(8,128)(2,1)}, u32[]{:S(2)}) copy-start(bf16[1,1024,1024]{2,1,0:T(8,128)(2,1)} %all-gather.3.cloned.1.call-done) | copy-start | bytes 6291460
  70.5 6.8 %collective-permute-start = (f32[24,1024]{1,0:T(8,128)S(1)}, f32[24,1024]{1,0:T(8,128)S(1)}, u32[]{:S(2)}, u32[]{:S(2)}) collective-permute-start(f32[24,1024]{1,0:T(8,128)S(1)} %fusion.31), channel_id=1, source_target_pairs={{4,0},{8,4},{12,8},{5,1},{9,5},{13,9},{6,2},{10,6},{14,10},{7,3},{... | collective-permute-start | bytes 294920 | tf_op jit(solution)/shard_map/while/body/eval_jaxpr/ppermute | solution.py:10
  81.7 6.5 %collective-permute-start = (f32[24,1024]{1,0:T(8,128)S(1)}, f32[24,1024]{1,0:T(8,128)S(1)}, u32[]{:S(2)}, u32[]{:S(2)}) collective-permute-start(f32[24,1024]{1,0:T(8,128)S(1)} %fusion.31), channel_id=1, source_target_pairs={{4,0},{8,4},{12,8},{5,1},{9,5},{13,9},{6,2},{10,6},{14,10},{7,3},{... | collective-permute-start | bytes 294920 | tf_op jit(solution)/shard_map/while/body/eval_jaxpr/ppermute | solution.py:10
  92.5 6.5 %collective-permute-start = (f32[24,1024]{1,0:T(8,128)S(1)}, f32[24,1024]{1,0:T(8,128)S(1)}, u32[]{:S(2)}, u32[]{:S(2)}) collective-permute-start(f32[24,1024]{1,0:T(8,128)S(1)} %fusion.31), channel_id=1, source_target_pairs={{4,0},{8,4},{12,8},{5,1},{9,5},{13,9},{6,2},{10,6},{14,10},{7,3},{... | collective-permute-start | bytes 294920 | tf_op jit(solution)/shard_map/while/body/eval_jaxpr/ppermute | solution.py:10
Sparse Core Ops, SparseCore 0:
  9.6 25.5 all-gather.2
  36.7 22.8 all-gather.4
where the time goes:
time: 107 us
  waiting for transfers between devices  42.5 us (40%)
  matrix products  22.8 us (21%)
  blocking collectives  22.6 us (21%)
  between operations  14.1 us (13%)
  starting transfers between devices  3.94 us (4%)
    all_gather x1, waiting for transfers between devices, shards(): lax.all_gather(lower_coupling, ('tile', 'arrow'), axis=2, tiled=True)  24.4 us
    psum x1, blocking collectives, shards(): arrow_sum = lax.psum(local_part, 'tm')  20.3 us
    ppermute x3, waiting for transfers between devices, from_behind(): return lax.ppermute(block, axis, route)  16 us
    dot_general x3, matrix products, one_turn(): outgoing = jnp.dot(residual, coupling_wide, precision=highest)  13 us
    dot_general x1, matrix products, shards(): jnp.dot(inverse_full[0], lower_full[0], preferred_element_type=jnp.float32)  6.5 us
    ppermute x3, starting transfers between devices, from_behind(): return lax.ppermute(block, axis, route)  3.86 us
    all_gather x1, blocking collectives, shards(): slab_full = lax.all_gather(arrow_slab, 'arrow', axis=1, tiled=True)  2.21 us
  transfers between devices with their start and end apart: 5, of which 5 were waited for; matrix products, arithmetic and copies ran while one was open for 3% of the time, Pallas kernels for 0%

commit v1 on v0

--- a/solution.py
+++ b/solution.py
@@ -24,7 +24,11 @@
     slab_wide = slab_full[0].astype(jnp.float32)
     block_rows = forward_blocks[0]
     local_part = jnp.dot(block_rows, slab_wide.T, precision=highest)
-    arrow_sum = lax.psum(local_part, "tm")
+    n_slots = lax.axis_size("tm")
+    arrow_sum = local_part
+    for ix in [src_i for src_i in (1, 2, 4, 8, 16) if src_i < n_slots]:
+        k_now = lax.ppermute(arrow_sum, "tm", [(rr, rr ^ ix) for rr in range(n_slots)])
+        arrow_sum = arrow_sum + k_now
     arrow_forward = jnp.dot(arrow_rhs - arrow_sum, arrow_inverse.T, precision=highest)
     arrow_solution = jnp.dot(arrow_forward, arrow_inverse, precision=highest)
     arrow_term = jnp.dot(arrow_solution, slab_wide, precision=highest)

time: 107 us -> 107 us (level)
  blocking collectives: 22.6 us -> 2.21 us
  waiting for transfers between devices: 42.5 us -> 56.7 us
  starting transfers between devices: 3.94 us -> 9.95 us
    psum x1 -> x0, blocking collectives: 20.3 us -> none  [shards(): arrow_sum = lax.psum(local_part, 'tm')]
    all_gather x1, waiting for transfers between devices: 0.68 us -> 12.6 us  [shards(): lax.all_gather(diag_inverse, ('tile', 'arrow'), axis=2, tiled=True)]
    ppermute x0 -> x2, starting transfers between devices: none -> 6.01 us  [shards(): lax.ppermute(arrow_sum, 'tm', [(rr, rr ^ ix) for rr in range(n_slots)])]
    ppermute x0 -> x2, waiting for transfers between devices: none -> 2.4 us  [shards(): lax.ppermute(arrow_sum, 'tm', [(rr, rr ^ ix) for rr in range(n_slots)])]
  transfers between devices with their start and end apart: 5 -> 7, of which waited for: 5 -> 7; matrix products, arithmetic and copies ran while one was open for 3% -> 3% of each run, Pallas kernels for 0% -> 0%
where the time goes in v1:
time: 107 us
  waiting for transfers between devices  56.7 us (53%)
  matrix products  22.8 us (21%)
  between operations  14.1 us (13%)
  starting transfers between devices  9.95 us (9%)
  blocking collectives  2.21 us (2%)
    all_gather x1, waiting for transfers between devices, shards(): lax.all_gather(lower_coupling, ('tile', 'arrow'), axis=2, tiled=True)  24.4 us
    ppermute x3, waiting for transfers between devices, from_behind(): return lax.ppermute(block, axis, route)  16 us
    dot_general x3, matrix products, one_turn(): outgoing = jnp.dot(residual, coupling_wide, precision=highest)  13 us
    all_gather x1, waiting for transfers between devices, shards(): lax.all_gather(diag_inverse, ('tile', 'arrow'), axis=2, tiled=True)  12.6 us
    dot_general x1, matrix products, shards(): jnp.dot(inverse_full[0], lower_full[0], preferred_element_type=jnp.float32)  6.5 us
    ppermute x2, starting transfers between devices, shards(): lax.ppermute(arrow_sum, 'tm', [(rr, rr ^ ix) for rr in range(n_slots)])  6.01 us
    ppermute x3, starting transfers between devices, from_behind(): return lax.ppermute(block, axis, route)  3.86 us
    ppermute x2, waiting for transfers between devices, shards(): lax.ppermute(arrow_sum, 'tm', [(rr, rr ^ ix) for rr in range(n_slots)])  2.4 us
  transfers between devices with their start and end apart: 7, of which 7 were waited for; matrix products, arithmetic and copies ran while one was open for 3% of the time, Pallas kernels for 0%

profile of v1, /device:TPU:0, one launch (start us, length us, event | category | flops | bytes accessed | tf_op | source)
XLA Modules:
  0.0 106.9 jit_solution(15334228126374110423)
XLA Ops:
  7.2 0.0 copy-start
  7.2 0.0 copy-start.2
  7.2 0.0 all-gather.3.cloned.1.call-start
  7.2 0.7 all-gather.3.cloned.1.call-update
  7.9 0.0 all-gather.5.cloned.1.call-start
  8.0 0.7 all-gather.5.cloned.1.call-update
  8.7 2.2 %all_gather.9 = bf16[1,64,1024]{2,1,0:T(8,128)(2,1)S(1)} all-gather(bf16[1,32,1024]{2,1,0:T(8,128)(2,1)} %param.13), channel_id=1, replica_groups=mesh['groups'=2,'tm'=4,'tile'=2,'arrow'=2] {'arrow'}, dimensions={1}, use_global_device_ids=true | all-gather | bytes 196608 | tf_op jit(solution)/shard_map/all_gather | solution.py:23
  10.9 1.1 fusion.15
  11.9 3.0 %collective-permute-start.1 = (f32[24,64]{1,0:T(8,128)S(1)}, f32[24,64]{1,0:T(8,128)S(1)}, u32[]{:S(2)}, u32[]{:S(2)}) collective-permute-start(f32[24,64]{1,0:T(8,128)S(1)} %fusion.15), channel_id=1, source_target_pairs={{0,4},{4,0},{8,12},{12,8},{1,5},{5,1},{9,13},{13,9},{2,6},{6,2},{1... | collective-permute-start | bytes 18440 | tf_op jit(solution)/shard_map/ppermute | solution.py:30
  14.9 1.7 %collective-permute-done.1 = f32[24,64]{1,0:T(8,128)S(1)} collective-permute-done((f32[24,64]{1,0:T(8,128)S(1)}, f32[24,64]{1,0:T(8,128)S(1)}, u32[]{:S(2)}, u32[]{:S(2)}) %collective-permute-start.1) | collective-permute-done | bytes 6176 | tf_op jit(solution)/shard_map/ppermute | solution.py:30
  16.6 3.0 %collective-permute-start.2 = (f32[24,64]{1,0:T(8,128)S(1)}, f32[24,64]{1,0:T(8,128)S(1)}, u32[]{:S(2)}, u32[]{:S(2)}) collective-permute-start(f32[24,64]{1,0:T(8,128)S(1)} %add.12), channel_id=1, source_target_pairs={{0,8},{4,12},{8,0},{12,4},{1,9},{5,13},{9,1},{13,5},{2,10},{6,14},... | collective-permute-start | bytes 18440 | tf_op jit(solution)/shard_map/ppermute | solution.py:30
  19.6 0.9 broadcast_multiply_fusion
  20.6 0.7 collective-permute-done.2
  21.3 0.0 copy-done
  21.3 0.9 fusion.18
  22.2 0.1 fusion.21
  22.4 0.0 copy-done.2
  22.4 0.0 copy-start.3
  22.4 0.2 convolution_subtract_fusion
  22.6 12.6 %all-gather.3.cloned.1.call-done = bf16[1,1024,1024]{2,1,0:T(8,128)(2,1)} async-done(((bf16[1,1024,256]{2,1,0:T(8,128)(2,1)}), bf16[1,1024,1024]{2,1,0:T(8,128)(2,1)}) %all-gather.3.cloned.1.call-update) | async-done | bytes 2097168 | tf_op jit(solution)/shard_map/all_gather | solution.py:37
  35.1 24.4 %all-gather.5.cloned.1.call-done = bf16[1,1024,1024]{2,1,0:T(8,128)(2,1)} async-done(((bf16[1,1024,256]{2,1,0:T(8,128)(2,1)}), bf16[1,1024,1024]{2,1,0:T(8,128)(2,1)}) %all-gather.5.cloned.1.call-update) | async-done | bytes 2097168 | tf_op jit(solution)/shard_map/all_gather | solution.py:38
  59.6 6.5 %convert_convert_fusion = f32[1024,1024]{1,0:T(8,128)} fusion(bf16[1,1024,1024]{2,1,0:T(8,128)(2,1)} %all-gather.5.cloned.1.call-done, bf16[1,1024,1024]{2,1,0:T(8,128)(2,1)} %all-gather.3.cloned.1.call-done), kind=kOutput, calls=%fused_computation.7 | convolution fusion | flops 2149580800 | bytes 8388608 | tf_op jit(solution)/shard_map/dot_general | solution.py:40
  66.1 0.0 copy-done.3
  66.1 0.0 copy-start.1
  66.1 32.9 %while.10 = (s32[]{:T(128)}, f32[24,1024]{1,0:T(8,128)S(1)}, f32[24,1024]{1,0:T(8,128)S(1)}, f32[1024,1024]{1,0:T(8,128)}, f32[24,1024]{1,0:T(8,128)S(1)}, /*index=5*/s32[]{:T(128)}) while((s32[]{:T(128)}, f32[24,1024]{1,0:T(8,128)S(1)}, f32[24,1024]{1,0:T(8,128)S(1)}, f32[1024,1024]{1,0:T(8,128)}, f32[24,1024]{1,0:T(8,128)S(1)}, ...), condition=%wide.region_1.0_spmd, body=%wide.region_0.0_spmd.sunk | while | flops 302039040 | bytes 5177453 | solution.py:52
  66.1 4.4 %fusion.32 = f32[24,1024]{1,0:T(8,128)S(1)} fusion(f32[1024,1024]{1,0:T(8,128)} %get-tuple-element.86, f32[24,1024]{1,0:T(8,128)S(1)} %get-tuple-element.85, f32[24,1024]{1,0:T(8,128)S(1)} %get-tuple-element.78), kind=kOutput, calls=%fused_computation.clone.1 | convolution fusion | flops 302014464 | bytes 4489216 | tf_op jit(solution)/shard_map/while/body/eval_jaxpr/dot_general | solution.py:49
  70.5 1.3 %collective-permute-start = (f32[24,1024]{1,0:T(8,128)S(1)}, f32[24,1024]{1,0:T(8,128)S(1)}, u32[]{:S(2)}, u32[]{:S(2)}) collective-permute-start(f32[24,1024]{1,0:T(8,128)S(1)} %fusion.32), channel_id=1, source_target_pairs={{4,0},{8,4},{12,8},{5,1},{9,5},{13,9},{6,2},{10,6},{14,10},{7,3},{... | collective-permute-start | bytes 294920 | tf_op jit(solution)/shard_map/while/body/eval_jaxpr/ppermute | solution.py:10
  71.8 5.6 %collective-permute-done = f32[24,1024]{1,0:T(8,128)S(1)} collective-permute-done((f32[24,1024]{1,0:T(8,128)S(1)}, f32[24,1024]{1,0:T(8,128)S(1)}, u32[]{:S(2)}, u32[]{:S(2)}) %collective-permute-start) | collective-permute-done | bytes 98336 | tf_op jit(solution)/shard_map/while/body/eval_jaxpr/ppermute | solution.py:10
  77.4 4.3 %fusion.32 = f32[24,1024]{1,0:T(8,128)S(1)} fusion(f32[1024,1024]{1,0:T(8,128)} %get-tuple-element.86, f32[24,1024]{1,0:T(8,128)S(1)} %get-tuple-element.85, f32[24,1024]{1,0:T(8,128)S(1)} %get-tuple-element.78), kind=kOutput, calls=%fused_computation.clone.1 | convolution fusion | flops 302014464 | bytes 4489216 | tf_op jit(solution)/shard_map/while/body/eval_jaxpr/dot_general | solution.py:49
  81.7 1.3 %collective-permute-start = (f32[24,1024]{1,0:T(8,128)S(1)}, f32[24,1024]{1,0:T(8,128)S(1)}, u32[]{:S(2)}, u32[]{:S(2)}) collective-permute-start(f32[24,1024]{1,0:T(8,128)S(1)} %fusion.32), channel_id=1, source_target_pairs={{4,0},{8,4},{12,8},{5,1},{9,5},{13,9},{6,2},{10,6},{14,10},{7,3},{... | collective-permute-start | bytes 294920 | tf_op jit(solution)/shard_map/while/body/eval_jaxpr/ppermute | solution.py:10
  83.0 5.2 %collective-permute-done = f32[24,1024]{1,0:T(8,128)S(1)} collective-permute-done((f32[24,1024]{1,0:T(8,128)S(1)}, f32[24,1024]{1,0:T(8,128)S(1)}, u32[]{:S(2)}, u32[]{:S(2)}) %collective-permute-start) | collective-permute-done | bytes 98336 | tf_op jit(solution)/shard_map/while/body/eval_jaxpr/ppermute | solution.py:10
  88.2 4.3 %fusion.32 = f32[24,1024]{1,0:T(8,128)S(1)} fusion(f32[1024,1024]{1,0:T(8,128)} %get-tuple-element.86, f32[24,1024]{1,0:T(8,128)S(1)} %get-tuple-element.85, f32[24,1024]{1,0:T(8,128)S(1)} %get-tuple-element.78), kind=kOutput, calls=%fused_computation.clone.1 | convolution fusion | flops 302014464 | bytes 4489216 | tf_op jit(solution)/shard_map/while/body/eval_jaxpr/dot_general | solution.py:49
  92.5 1.3 %collective-permute-start = (f32[24,1024]{1,0:T(8,128)S(1)}, f32[24,1024]{1,0:T(8,128)S(1)}, u32[]{:S(2)}, u32[]{:S(2)}) collective-permute-start(f32[24,1024]{1,0:T(8,128)S(1)} %fusion.32), channel_id=1, source_target_pairs={{4,0},{8,4},{12,8},{5,1},{9,5},{13,9},{6,2},{10,6},{14,10},{7,3},{... | collective-permute-start | bytes 294920 | tf_op jit(solution)/shard_map/while/body/eval_jaxpr/ppermute | solution.py:10
  93.8 5.2 %collective-permute-done = f32[24,1024]{1,0:T(8,128)S(1)} collective-permute-done((f32[24,1024]{1,0:T(8,128)S(1)}, f32[24,1024]{1,0:T(8,128)S(1)}, u32[]{:S(2)}, u32[]{:S(2)}) %collective-permute-start) | collective-permute-done | bytes 98336 | tf_op jit(solution)/shard_map/while/body/eval_jaxpr/ppermute | solution.py:10
  99.0 0.0 copy-done.1
  99.0 1.0 fusion.11
  (5 shorter events, 0.0 us)
Async XLA Ops:
  7.2 14.2 %copy-start = (f32[64,64]{1,0:T(8,128)S(1)}, f32[64,64]{1,0:T(8,128)}, u32[]{:S(2)}) copy-start(f32[64,64]{1,0:T(8,128)} %param.14) | copy-start | bytes 49156
  7.2 15.2 %copy-start.2 = (f32[1,24,1024]{2,1,0:T(8,128)S(1)}, f32[1,24,1024]{2,1,0:T(8,128)}, u32[]{:S(2)}) copy-start(f32[1,24,1024]{2,1,0:T(8,128)} %param.9) | copy-start | bytes 294916
  7.2 28.0 %all-gather.3.cloned.1.call-start = ((), (), s32[]{:S(2)}) async-start(), calls=%async_computation | async-start | bytes 2621440 | tf_op jit(solution)/shard_map/all_gather | solution.py:37
  7.9 51.6 %all-gather.5.cloned.1.call-start = ((), (), s32[]{:S(2)}) async-start(), calls=%async_computation.1 | async-start | bytes 2621440 | tf_op jit(solution)/shard_map/all_gather | solution.py:38
  11.9 4.7 %collective-permute-start.1 = (f32[24,64]{1,0:T(8,128)S(1)}, f32[24,64]{1,0:T(8,128)S(1)}, u32[]{:S(2)}, u32[]{:S(2)}) collective-permute-start(f32[24,64]{1,0:T(8,128)S(1)} %fusion.15), channel_id=1, source_target_pairs={{0,4},{4,0},{8,12},{12,8},{1,5},{5,1},{9,13},{13,9},{2,6},{6,2},{1... | collective-permute-start | bytes 18440 | tf_op jit(solution)/shard_map/ppermute | solution.py:30
  16.6 4.7 %collective-permute-start.2 = (f32[24,64]{1,0:T(8,128)S(1)}, f32[24,64]{1,0:T(8,128)S(1)}, u32[]{:S(2)}, u32[]{:S(2)}) collective-permute-start(f32[24,64]{1,0:T(8,128)S(1)} %add.12), channel_id=1, source_target_pairs={{0,8},{4,12},{8,0},{12,4},{1,9},{5,13},{9,1},{13,5},{2,10},{6,14},... | collective-permute-start | bytes 18440 | tf_op jit(solution)/shard_map/ppermute | solution.py:30
  22.4 43.7 %copy-start.3 = (f32[24,64]{1,0:T(8,128)}, f32[24,64]{1,0:T(8,128)S(1)}, u32[]{:S(2)}) copy-start(f32[24,64]{1,0:T(8,128)S(1)} %fusion.21) | copy-start | bytes 18436
  66.1 33.0 %copy-start.1 = (bf16[1,1024,1024]{2,1,0:T(8,128)(2,1)S(1)}, bf16[1,1024,1024]{2,1,0:T(8,128)(2,1)}, u32[]{:S(2)}) copy-start(bf16[1,1024,1024]{2,1,0:T(8,128)(2,1)} %all-gather.3.cloned.1.call-done) | copy-start | bytes 6291460
  70.5 6.8 %collective-permute-start = (f32[24,1024]{1,0:T(8,128)S(1)}, f32[24,1024]{1,0:T(8,128)S(1)}, u32[]{:S(2)}, u32[]{:S(2)}) collective-permute-start(f32[24,1024]{1,0:T(8,128)S(1)} %fusion.32), channel_id=1, source_target_pairs={{4,0},{8,4},{12,8},{5,1},{9,5},{13,9},{6,2},{10,6},{14,10},{7,3},{... | collective-permute-start | bytes 294920 | tf_op jit(solution)/shard_map/while/body/eval_jaxpr/ppermute | solution.py:10
  81.7 6.5 %collective-permute-start = (f32[24,1024]{1,0:T(8,128)S(1)}, f32[24,1024]{1,0:T(8,128)S(1)}, u32[]{:S(2)}, u32[]{:S(2)}) collective-permute-start(f32[24,1024]{1,0:T(8,128)S(1)} %fusion.32), channel_id=1, source_target_pairs={{4,0},{8,4},{12,8},{5,1},{9,5},{13,9},{6,2},{10,6},{14,10},{7,3},{... | collective-permute-start | bytes 294920 | tf_op jit(solution)/shard_map/while/body/eval_jaxpr/ppermute | solution.py:10
  92.5 6.5 %collective-permute-start = (f32[24,1024]{1,0:T(8,128)S(1)}, f32[24,1024]{1,0:T(8,128)S(1)}, u32[]{:S(2)}, u32[]{:S(2)}) collective-permute-start(f32[24,1024]{1,0:T(8,128)S(1)} %fusion.32), channel_id=1, source_target_pairs={{4,0},{8,4},{12,8},{5,1},{9,5},{13,9},{6,2},{10,6},{14,10},{7,3},{... | collective-permute-start | bytes 294920 | tf_op jit(solution)/shard_map/while/body/eval_jaxpr/ppermute | solution.py:10
Sparse Core Ops, SparseCore 0:
  9.6 25.5 all-gather.2
  36.7 22.8 all-gather.4
